TPU v7x, 32 devices: a whole 2x2x4 slice. The times are simulated.
32 devices in a mesh: seq: 8 (over z, x), batch: 4 (over y, core).
Axes of the slice: x: 2, y: 2, z: 4, core: 2. Of those that a mesh axis runs over, the one named last changes fastest.
Arguments:
- signal: bfloat16 [65536, 512], P(('batch', 'seq')), parts along dimension 0, may hold values from -6 to 6
- kernel_weight_stack: bfloat16 [2, 1024, 1024], P(None, 'seq'), may hold values from -0.1875 to 0.1875
- blend_weight_stack: bfloat16 [2, 512, 512], P(None, 'seq'), may hold values from -0.25 to 0.25
Outputs:
- layer_outs: bfloat16 [2, 65536, 512], P(None, ('batch', 'seq')), parts along dimension 1
There are 4 independent parts, one for each index of `batch`. A program takes and returns all parts, laid end to end along the dimension named above; an argument that names none is the same for every part. Nothing has to cross between parts.
All inputs are finite; a program needn't handle non-finite values.
Results may differ from a plain program's by a relative error of at most 0.0043.
Values may be sent and summed in bfloat16 or wider, within the bound.
A program may use at most 64 MiB of HBM per device.

v0:
```python
import jax
import jax.numpy as jnp
from jax import lax
from jax.sharding import PartitionSpec as P


def shifted(block, axis, distance):
    devices = range(lax.axis_size(axis))
    route = [(i - distance, i) for i in devices if i - distance in devices]
    return lax.ppermute(block, axis, route)


def per_device(signal, kernel_weight_stack, blend_weight_stack):
    layers = kernel_weight_stack.shape[0]
    channels = signal.shape[1]
    rows = signal.shape[0]
    hidden = signal
    layer_outs = []
    for layer_position_index in range(layers):
        layer_spacing = rows // 2 << layer_position_index
        layer_kernel_weight, layer_blend_weight = (
            lax.all_gather(kernel_weight_stack[layer_position_index], "seq", axis=0, tiled=True),
            lax.all_gather(blend_weight_stack[layer_position_index], "seq", axis=0, tiled=True),
        )
        if layer_spacing < rows:
            arrived = shifted(hidden[rows - layer_spacing :], "seq", 1)
            delayed = jnp.concatenate([arrived, hidden[: rows - layer_spacing]], axis=0)
        else:
            delayed = shifted(hidden, "seq", layer_spacing // rows)
        current = jnp.dot(
            hidden, layer_kernel_weight[channels:], preferred_element_type=jnp.float32
        )
        preact = current + jnp.dot(
            delayed, layer_kernel_weight[:channels], preferred_element_type=jnp.float32
        )
        gated_output = (
            jnp.tanh(preact[:, :channels]) * jax.nn.sigmoid(preact[:, channels:])
        ).astype(jnp.bfloat16)
        mix_out = jnp.dot(gated_output, layer_blend_weight, preferred_element_type=jnp.float32)
        hidden = (hidden.astype(jnp.float32) + mix_out).astype(jnp.bfloat16)
        layer_outs.append(hidden)
    return jnp.stack(layer_outs)


def solution(mesh):
    return jax.shard_map(
        per_device,
        mesh=mesh,
        in_specs=(P(("batch", "seq"), None), P(None, "seq", None), P(None, "seq", None)),
        out_specs=P(None, ("batch", "seq"), None),
        check_vma=False,
    )
```

profile of v0, /device:TPU:0, one launch (start us, length us, event | category | flops | bytes accessed | tf_op | source)
XLA Modules:
  0.0 204.0 jit_solution(920687612548163553)
XLA Ops:
  6.5 0.0 copy-start
  6.5 0.0 copy-start.4
  6.5 0.0 all-gather.7.cloned.1.call-start
  6.5 2.0 fusion.24
  8.6 0.0 all-gather.7.cloned.1.call-update
  8.6 0.0 all-gather.9.cloned.1.call-start
  8.6 2.6 %fusion.23 = (bf16[1024,512]{1,0:T(8,128)(2,1)}, bf16[1024,512]{1,0:T(8,128)(2,1)S(1)}) fusion(bf16[2048,512]{1,0:T(8,128)(2,1)} %param.3), kind=kLoop, calls=%fused_computation.34 | loop fusion | bytes 4194304 | tf_op jit(solution)/shard_map/slice | solution.py:26
  11.3 5.8 %collective-permute-start = (bf16[1024,512]{1,0:T(8,128)(2,1)}, bf16[1024,512]{1,0:T(8,128)(2,1)}, u32[]{:S(2)}, u32[]{:S(2)}) collective-permute-start(bf16[1024,512]{1,0:T(8,128)(2,1)} %get-tuple-element.5), channel_id=1, source_target_pairs={{0,4},{4,8},{8,12},{12,16},{16,20},{20,24},{24,28},{1,5},{5,9},{9,... | collective-permute-start | bytes 3145736 | tf_op jit(solution)/shard_map/ppermute | solution.py:10
  17.1 0.0 all-gather.9.cloned.1.call-update
  17.1 0.0 copy-done.4
  17.2 69.9 %all-gather.1 = bf16[1,512,512]{2,1,0:T(8,128)(2,1)} all-gather(bf16[1,64,512]{2,1,0:T(8,128)(2,1)S(1)} %get-tuple-element.10), channel_id=3, replica_groups=mesh['seq'=8,'batch'=4] {'seq'}, dimensions={1}, use_global_device_ids=true | all-gather | bytes 589824 | tf_op jit(solution)/shard_map/all_gather | solution.py:23
  87.1 0.0 all-gather.7.cloned.1.call-done
  87.1 0.0 copy-done
  87.1 0.0 copy-start.2
  87.1 3.7 %fusion.17 = f32[2048,1024]{1,0:T(8,128)S(1)} fusion(bf16[2048,512]{1,0:T(8,128)(2,1)S(1)} %copy-done, bf16[1,1024,1024]{2,1,0:T(8,128)(2,1)} %all-gather.7.cloned.1.call-done), kind=kOutput, calls=%fused_computation.28 | convolution fusion | flops 2147483648 | bytes 11534336 | tf_op jit(solution)/shard_map/dot_general | solution.py:30
  90.8 0.0 collective-permute-done
  90.8 0.0 copy-done.2
  90.8 0.0 copy-start.3
  90.8 3.6 %convolution_add_fusion.1 = f32[2048,1024]{1,0:T(8,128)S(1)} fusion(f32[2048,1024]{1,0:T(8,128)S(1)} %fusion.17, bf16[1024,512]{1,0:T(8,128)(2,1)S(1)} %get-tuple-element.6, bf16[1024,512]{1,0:T(8,128)(2,1)} %collective-permute-done, bf16[1,1024,1024]{2,1,0:T(8,128)(2,1)S(1)} %copy-done.2), kind=kOutput, calls=%fused_computation.18 | convolution fusion | flops 2153775104 | bytes 19922944 | tf_op jit(solution)/shard_map/dot_general | solution.py:33
  94.4 0.0 copy-done.3
  94.5 3.0 %add_convert_fusion.1 = bf16[2048,512]{1,0:T(8,128)(2,1)} fusion(bf16[2048,512]{1,0:T(8,128)(2,1)S(1)} %copy-done, f32[2048,1024]{1,0:T(8,128)S(1)} %convolution_add_fusion.1, bf16[1,512,512]{2,1,0:T(8,128)(2,1)S(1)} %copy-done.3), kind=kOutput, calls=%fused_computation.14 | convolution fusion | flops 1082130432 | bytes 13107200 | tf_op jit(solution)/shard_map/dot_general | solution.py:39
  97.5 1.4 collective-permute-start.1
  98.9 84.1 %all-gather.3 = bf16[1,512,512]{2,1,0:T(8,128)(2,1)S(1)} all-gather(bf16[1,64,512]{2,1,0:T(8,128)(2,1)S(1)} %get-tuple-element.9), channel_id=5, replica_groups=mesh['seq'=8,'batch'=4] {'seq'}, dimensions={1}, use_global_device_ids=true | all-gather | bytes 589824 | tf_op jit(solution)/shard_map/all_gather | solution.py:23
  183.0 0.0 all-gather.9.cloned.1.call-done
  183.0 0.0 copy-start.1
  183.0 4.5 %fusion.16 = f32[2048,1024]{1,0:T(8,128)S(1)} fusion(bf16[2048,512]{1,0:T(8,128)(2,1)} %add_convert_fusion.1, bf16[1,1024,1024]{2,1,0:T(8,128)(2,1)} %all-gather.9.cloned.1.call-done), kind=kOutput, calls=%fused_computation.25 | convolution fusion | flops 2147483648 | bytes 11534336 | tf_op jit(solution)/shard_map/dot_general | solution.py:30
  187.4 0.0 collective-permute-done.1
  187.5 0.0 copy-done.1
  187.5 2.5 %convolution_add_fusion = f32[2048,1024]{1,0:T(8,128)S(1)} fusion(f32[2048,1024]{1,0:T(8,128)S(1)} %fusion.16, bf16[2048,512]{1,0:T(8,128)(2,1)S(1)} %collective-permute-done.1, bf16[1,1024,1024]{2,1,0:T(8,128)(2,1)S(1)} %copy-done.1), kind=kOutput, calls=%fused_computation.17 | convolution fusion | flops 2149580800 | bytes 19922944 | tf_op jit(solution)/shard_map/dot_general | solution.py:33
  190.0 3.2 %fusion.10 = bf16[1,2048,512]{2,1,0:T(8,128)(2,1)S(1)} fusion(bf16[2048,512]{1,0:T(8,128)(2,1)} %add_convert_fusion.1, f32[2048,1024]{1,0:T(8,128)S(1)} %convolution_add_fusion, bf16[1,512,512]{2,1,0:T(8,128)(2,1)S(1)} %all-gather.3), kind=kOutput, calls=%fused_computation.19 | convolution fusion | flops 1082130432 | bytes 13107200 | tf_op jit(solution)/shard_map/dot_general | solution.py:39
  193.2 4.0 %pad_maximum_fusion = bf16[2,2048,512]{2,1,0:T(8,128)(2,1)} fusion(bf16[1,2048,512]{2,1,0:T(8,128)(2,1)S(1)} %fusion.10, bf16[1,2048,512]{2,1,0:T(8,128)(2,1)} %bitcast.3), kind=kLoop, calls=%fused_computation.12 | loop fusion | flops 2097152 | bytes 8388608 | tf_op jit(solution)/shard_map/stack | solution.py:42
  (1 shorter events, 0.0 us)
Async XLA Ops:
  6.5 80.5 %copy-start = (bf16[2048,512]{1,0:T(8,128)(2,1)S(1)}, bf16[2048,512]{1,0:T(8,128)(2,1)}, u32[]{:S(2)}) copy-start(bf16[2048,512]{1,0:T(8,128)(2,1)} %param.3) | copy-start | bytes 6291460
  6.5 10.6 %copy-start.4 = (bf16[2,64,512]{2,1,0:T(8,128)(2,1)S(1)}, bf16[2,64,512]{2,1,0:T(8,128)(2,1)}, u32[]{:S(2)}) copy-start(bf16[2,64,512]{2,1,0:T(8,128)(2,1)} %param.5) | copy-start | bytes 393220
  6.5 80.5 %all-gather.7.cloned.1.call-start = ((), (), s32[]{:S(2)}) async-start(), calls=%async_computation | async-start | bytes 2359296 | tf_op jit(solution)/shard_map/all_gather | solution.py:22
  8.6 174.4 %all-gather.9.cloned.1.call-start = ((), (), s32[]{:S(2)}) async-start(), calls=%async_computation.1 | async-start | bytes 2359296 | tf_op jit(solution)/shard_map/all_gather | solution.py:22
  11.3 79.5 %collective-permute-start = (bf16[1024,512]{1,0:T(8,128)(2,1)}, bf16[1024,512]{1,0:T(8,128)(2,1)}, u32[]{:S(2)}, u32[]{:S(2)}) collective-permute-start(bf16[1024,512]{1,0:T(8,128)(2,1)} %get-tuple-element.5), channel_id=1, source_target_pairs={{0,4},{4,8},{8,12},{12,16},{16,20},{20,24},{24,28},{1,5},{5,9},{9,... | collective-permute-start | bytes 3145736 | tf_op jit(solution)/shard_map/ppermute | solution.py:10
  87.1 3.7 %copy-start.2 = (bf16[1,1024,1024]{2,1,0:T(8,128)(2,1)S(1)}, bf16[1,1024,1024]{2,1,0:T(8,128)(2,1)}, u32[]{:S(2)}) copy-start(bf16[1,1024,1024]{2,1,0:T(8,128)(2,1)} %all-gather.7.cloned.1.call-done) | copy-start | bytes 6291460
  90.8 3.6 %copy-start.3 = (bf16[1,512,512]{2,1,0:T(8,128)(2,1)S(1)}, bf16[1,512,512]{2,1,0:T(8,128)(2,1)}, u32[]{:S(2)}) copy-start(bf16[1,512,512]{2,1,0:T(8,128)(2,1)} %all-gather.1) | copy-start | bytes 1572868
  97.5 90.0 %collective-permute-start.1 = (bf16[2048,512]{1,0:T(8,128)(2,1)}, bf16[2048,512]{1,0:T(8,128)(2,1)S(1)}, u32[]{:S(2)}, u32[]{:S(2)}) collective-permute-start(bf16[2048,512]{1,0:T(8,128)(2,1)} %add_convert_fusion.1), channel_id=1, source_target_pairs={{0,4},{4,8},{8,12},{12,16},{16,20},{20,24},{24,28},{1,5},{5,9},{9,... | collective-permute-start | bytes 6291464 | tf_op jit(solution)/shard_map/ppermute | solution.py:10
  183.0 4.5 %copy-start.1 = (bf16[1,1024,1024]{2,1,0:T(8,128)(2,1)S(1)}, bf16[1,1024,1024]{2,1,0:T(8,128)(2,1)}, u32[]{:S(2)}) copy-start(bf16[1,1024,1024]{2,1,0:T(8,128)(2,1)} %all-gather.9.cloned.1.call-done) | copy-start | bytes 6291460
Sparse Core Ops, SparseCore 0:
  9.5 65.5 all-gather.6
  77.3 62.8 all-gather.8
where the time goes:
time: 204 us
  blocking collectives  154 us (75%)
  matrix products  20.6 us (10%)
  between operations  13.5 us (7%)
  starting transfers between devices  7.27 us (4%)
  local copies, waits for them, and re-layouts  4.71 us (2%)
  other arithmetic  3.99 us (2%)
    all_gather x2, blocking collectives, per_device(): lax.all_gather(blend_weight_stack[layer_position_index], 'seq', axis=0, t...  154 us
    dot_general x2, matrix products, per_device(): jnp.dot(hidden, layer_kernel_weight[channels:], preferred_element_type=jn...  8.17 us
    ppermute x2, starting transfers between devices, shifted(): return lax.ppermute(block, axis, route)  7.22 us
    dot_general x2, matrix products, per_device(): jnp.dot(gated_output, layer_blend_weight, preferred_element_type=jnp.floa...  6.24 us
    dot_general x2, matrix products, per_device(): jnp.dot(delayed, layer_kernel_weight[:channels], preferred_element_type=j...  6.14 us
  transfers between devices with their start and end apart: 4, of which 0 were waited for; matrix products, arithmetic and copies ran while one was open for 9% of the time, Pallas kernels for 0%

commit v1 on v0

v1 whole, which is shorter than its diff:
```python
import functools

import jax
import jax.numpy as jnp
from jax import lax
from jax.experimental import pallas as pl
from jax.experimental.pallas import tpu as pltpu
from jax.sharding import PartitionSpec as P

MESH = pl.DeviceIdType.MESH
TILE = 256


def flip(index, bit):
    return index + bit - 2 * bit * ((index // bit) % 2)


def kernel(n, nb, gather_blend, sig, kw, bw, out, sbuf, hbuf, obuf, kfull, bfull,
           seq_s, seq_r, bat_s, bat_r, act_s, act_r, own_sem, load_sem, out_sem):
    i = lax.axis_index("seq")
    b = lax.axis_index("batch")
    rows = sig.shape[0]
    half = rows // 2
    layers = kw.shape[0]
    channels = sig.shape[1]
    masks = [nb >> (k + 1) for k in range(nb.bit_length() - 1)]

    load = pltpu.make_async_copy(sig, sbuf.at[pl.ds(3 * half, rows)], load_sem)
    load.start()

    barrier = pltpu.get_barrier_semaphore()

    def greet(d, _):
        pl.semaphore_signal(barrier, inc=1, device_id={"seq": lax.rem(i + d, n)}, device_id_type=MESH)
        return 0

    lax.fori_loop(1, n, greet, 0)
    for m in masks:
        pl.semaphore_signal(barrier, inc=1, device_id={"batch": flip(b, m)}, device_id_type=MESH)

    weights = [(kw, kfull)] + ([(bw, bfull)] if gather_blend else [])

    def cols(full, quarter):
        width = full.shape[2] // nb
        return pl.ds(pl.multiple_of(quarter * width, width), width)

    def shard(full, part, l, source, quarter):
        count = part.shape[1]
        return full.at[l, pl.ds(pl.multiple_of(source * count, count), count), cols(full, quarter)]

    def seq_copy(l, w, d):
        part, full = weights[w]
        return pltpu.make_async_remote_copy(
            src_ref=part.at[l, :, cols(full, b)],
            dst_ref=shard(full, part, l, i, b),
            send_sem=seq_s.at[l, w, d], recv_sem=seq_r.at[l, w, d],
            device_id={"seq": lax.rem(i + d, n)}, device_id_type=MESH)

    def own_copy(l, w):
        part, full = weights[w]
        return pltpu.make_async_copy(part.at[l, :, cols(full, b)], shard(full, part, l, i, b), own_sem.at[l, w])

    def bat_copy(l, w, m, o):
        part, full = weights[w]
        quarter = b
        for bit in masks:
            if o & bit:
                quarter = flip(quarter, bit)
        where = full.at[l, :, cols(full, quarter)]
        return pltpu.make_async_remote_copy(
            src_ref=where, dst_ref=where,
            send_sem=bat_s.at[l, w, o + m], recv_sem=bat_r.at[l, w, o + m],
            device_id={"batch": flip(b, m)}, device_id_type=MESH)

    def act_copy(k):
        source, slot, hop = ((half, 2, 1), (0, 1, 1), (half, 0, 2))[k]
        return hop, pltpu.make_async_remote_copy(
            src_ref=sig.at[pl.ds(source, half)], dst_ref=sbuf.at[pl.ds(slot * half, half)],
            send_sem=act_s.at[k], recv_sem=act_r.at[k],
            device_id={"seq": lax.rem(i + hop, n)}, device_id_type=MESH)

    def seq_start(l):
        def go(d, _):
            for w in range(len(weights)):
                seq_copy(l, w, d).start()
            return 0
        lax.fori_loop(1, n, go, 0)

    def seq_wait(l):
        def go(d, _):
            for w in range(len(weights)):
                seq_copy(l, w, d).wait_recv()
            return 0
        lax.fori_loop(1, n, go, 0)
        for w in range(len(weights)):
            own_copy(l, w).wait()

    for l in range(layers):
        for w in range(len(weights)):
            own_copy(l, w).start()
    if not gather_blend:
        blend = pltpu.make_async_copy(bw, bfull, own_sem.at[0, 1])
        blend.start()

    pl.semaphore_wait(barrier, n - 1 + len(masks))
    seq_start(0)
    for k in range(3):
        hop, copy = act_copy(k)
        pl.when(i + hop < n)(copy.start)
        pl.when(i < hop)(functools.partial(zero, sbuf, ((2, 1, 0)[k]) * half, half))
    seq_start(1)

    stages = [(m, [o for o in range(nb) if o % (2 * m) == 0 and all(o & x == 0 or x > m for x in masks)])
              for m in masks]

    def bat_start(l, s):
        m, held = stages[s]
        for o in held:
            for w in range(len(weights)):
                bat_copy(l, w, m, o).start()

    def bat_wait(l, s):
        m, held = stages[s]
        for o in held:
            for w in range(len(weights)):
                bat_copy(l, w, m, o).wait_recv()

    def layer(l, src, dst, shift, start, keep):
        def tile(t, _):
            at = pl.multiple_of(start + t * TILE, TILE)
            now = src[pl.ds(at + shift, TILE), :]
            late = src[pl.ds(at, TILE), :]
            pre = jnp.dot(late, kfull[l, :channels, :], preferred_element_type=jnp.float32)
            pre += jnp.dot(now, kfull[l, channels:, :], preferred_element_type=jnp.float32)
            gate = 0.5 * jnp.tanh(0.5 * pre[:, channels:]) + 0.5
            gated = (jnp.tanh(pre[:, :channels]) * gate).astype(jnp.bfloat16)
            mix = jnp.dot(gated, bfull[l], preferred_element_type=jnp.float32)
            dst[pl.ds(at, TILE), :] = (now.astype(jnp.float32) + mix).astype(jnp.bfloat16)
            return 0
        lax.fori_loop(0, half // TILE, tile, 0, unroll=2)
        if keep is not None:
            copy = pltpu.make_async_copy(
                dst.at[pl.ds(start, half)], out.at[l, pl.ds(keep * half, half)], out_sem.at[l, keep])
            copy.start()
            return [copy]
        return []

    def act_wait(k):
        hop, copy = act_copy(k)
        pl.when(i >= hop)(copy.wait_recv)

    seq_wait(0)
    for s in range(len(stages)):
        bat_start(0, s)
        bat_wait(0, s)
    load.wait()
    if not gather_blend:
        blend.wait()
    done = layer(0, sbuf, hbuf, half, 3 * half, 1)
    seq_wait(1)
    bat_start(1, 0)
    act_wait(0)
    done += layer(0, sbuf, hbuf, half, 2 * half, 0)
    for s in range(1, len(stages)):
        bat_wait(1, s - 1)
        bat_start(1, s)
    act_wait(1)
    done += layer(0, sbuf, hbuf, half, half, None)
    bat_wait(1, len(stages) - 1)
    done += layer(1, hbuf, obuf, rows, half, 1)
    act_wait(2)
    done += layer(0, sbuf, hbuf, half, 0, None)
    done += layer(1, hbuf, obuf, rows, 0, 0)

    def seq_sent(d, _):
        for l in range(layers):
            for w in range(len(weights)):
                seq_copy(l, w, d).wait_send()
        return 0

    lax.fori_loop(1, n, seq_sent, 0)
    for l in range(layers):
        for m, held in stages:
            for o in held:
                for w in range(len(weights)):
                    bat_copy(l, w, m, o).wait_send()
    for k in range(3):
        hop, copy = act_copy(k)
        pl.when(i + hop < n)(copy.wait_send)
    for copy in done:
        copy.wait()


def zero(ref, start, count):
    ref[pl.ds(start, count), :] = jnp.zeros((count, ref.shape[1]), ref.dtype)


def per_device(n, nb, signal, kernel_weight_stack, blend_weight_stack):
    rows, channels = signal.shape
    layers, part_rows, width = kernel_weight_stack.shape
    gather_blend = blend_weight_stack.shape[1] % 16 == 0
    if not gather_blend:
        blend_weight_stack = lax.all_gather(blend_weight_stack, "seq", axis=1, tiled=True)
    half = rows // 2
    dma = pltpu.SemaphoreType.DMA
    any_space = pl.BlockSpec(memory_space=pl.ANY)
    return pl.pallas_call(
        functools.partial(kernel, n, nb, gather_blend),
        out_shape=jax.ShapeDtypeStruct((layers, rows, channels), signal.dtype),
        in_specs=[any_space] * 3,
        out_specs=any_space,
        scratch_shapes=[
            pltpu.VMEM((5 * half, channels), signal.dtype),
            pltpu.VMEM((4 * half, channels), signal.dtype),
            pltpu.VMEM((rows, channels), signal.dtype),
            pltpu.VMEM((layers, n * part_rows, width), signal.dtype),
            pltpu.VMEM((layers, channels, channels), signal.dtype),
            dma((layers, 2, n)), dma((layers, 2, n)),
            dma((layers, 2, nb)), dma((layers, 2, nb)),
            dma((3,)), dma((3,)),
            dma((layers, 2)), dma, dma((layers, 2)),
        ],
        compiler_params=pltpu.CompilerParams(
            collective_id=0, has_side_effects=True, vmem_limit_bytes=48 * 2**20),
        cost_estimate=pl.CostEstimate(
            flops=3 * 2 * rows * channels * (2 * width + channels),
            bytes_accessed=2 * rows * channels * 2 * 3, transcendentals=3 * rows * width),
    )(signal, kernel_weight_stack, blend_weight_stack)


def solution(mesh):
    return jax.shard_map(
        functools.partial(per_device, mesh.shape["seq"], mesh.shape["batch"]),
        mesh=mesh,
        in_specs=(P(("batch", "seq"), None), P(None, "seq", None), P(None, "seq", None)),
        out_specs=P(None, ("batch", "seq"), None),
        check_vma=False,
    )
```

time: 204 us -> 140 us (0.69)
  the two profiles are of different devices: /device:TPU:0 before, /device:TPU:26 now
where the time goes in v1:
time: 140 us
  Pallas kernels  132 us (94%)
  local copies, waits for them, and re-layouts  8.01 us (6%)
    pallas_call x1, Pallas kernels, per_device(): pl.pallas_call(functools.partial(kernel, n, nb, gather_blend), out_shape=...  132 us
    unnamed x7, local copies, waits for them, and re-layouts  8.01 us

profile of v1, /device:TPU:26, one launch (start us, length us, event | category | flops | bytes accessed | tf_op | source)
XLA Modules:
  0.0 139.7 jit_solution(11287864690457272903)
XLA Ops:
  0.0 0.0 copy-start
  0.0 1.6 %copy-done = bf16[2048,512]{1,0:T(8,128)(2,1)S(1)} copy-done((bf16[2048,512]{1,0:T(8,128)(2,1)S(1)}, bf16[2048,512]{1,0:T(8,128)(2,1)}, u32[]{:S(2)}) %copy-start) | copy-done | bytes 2097176
  1.6 0.0 copy-start.1
  1.6 1.0 copy-done.1
  2.6 0.0 copy-start.2
  2.6 0.9 copy-done.2
  3.5 131.7 %shard_map.37 = bf16[2,2048,512]{2,1,0:T(8,128)(2,1)} custom-call(bf16[2048,512]{1,0:T(8,128)(2,1)S(1)} %copy-done, bf16[2,128,1024]{2,1,0:T(8,128)(2,1)S(1)} %copy-done.1, bf16[2,64,512]{2,1,0:T(8,128)(2,1)S(1)} %copy-done.2), custom_call_target="tpu_custom_call" | custom-call | flops 16106127360 | bytes 12582912 | tf_op jit(solution)/shard_map/pallas_call | solution.py:207
  135.2 4.5 %copy.5 = bf16[2,2048,512]{2,1,0:T(8,128)(2,1)} copy(bf16[2,2048,512]{2,1,0:T(8,128)(2,1)} %shard_map.37) | data formatting | bytes 8388608
Async XLA Ops:
  0.0 1.6 %copy-start = (bf16[2048,512]{1,0:T(8,128)(2,1)S(1)}, bf16[2048,512]{1,0:T(8,128)(2,1)}, u32[]{:S(2)}) copy-start(bf16[2048,512]{1,0:T(8,128)(2,1)} %sig.1) | copy-start | bytes 6291460
  1.6 1.0 copy-start.1
  2.6 0.9 copy-start.2

commit v2 on v1

v2 whole, which is shorter than its diff:
```python
import functools

import jax
import jax.numpy as jnp
from jax import lax
from jax.experimental import pallas as pl
from jax.experimental.pallas import tpu as pltpu
from jax.sharding import PartitionSpec as P

MESH = pl.DeviceIdType.MESH
TILE = 256
CHUNKS = 2


def flip(index, bit):
    return index + bit - 2 * bit * ((index // bit) % 2)


def kernel(n, nb, gather_blend, sig, kw, bw, out, sbuf, hbuf, obuf, kfull, bfull,
           seq_s, seq_r, par_s, par_r, bat_s, bat_r, act_s, act_r, own_sem, load_sem, out_sem):
    i = lax.axis_index("seq")
    b = lax.axis_index("batch")
    rows = sig.shape[0]
    half = rows // 2
    chunk = half // CHUNKS
    layers = kw.shape[0]
    channels = sig.shape[1]
    masks = [nb >> (k + 1) for k in range(nb.bit_length() - 1)]
    pairs = n // 2
    pair, side = i // 2, i % 2
    partner = flip(i, 1)

    load = pltpu.make_async_copy(sig, sbuf.at[pl.ds(3 * half, rows)], load_sem)
    load.start()

    barrier = pltpu.get_barrier_semaphore()

    def greet(d, _):
        pl.semaphore_signal(barrier, inc=1, device_id={"seq": lax.rem(i + d, n)}, device_id_type=MESH)
        return 0

    lax.fori_loop(1, n, greet, 0)
    for m in masks:
        pl.semaphore_signal(barrier, inc=1, device_id={"batch": flip(b, m)}, device_id_type=MESH)

    weights = [(kw, kfull)] + ([(bw, bfull)] if gather_blend else [])
    both = range(len(weights))

    def cols(full, quarter):
        width = full.shape[-1] // nb
        return pl.ds(pl.multiple_of(quarter * width, width), width)

    def seq_copy(l, w, d):
        part, full = weights[w]
        return pltpu.make_async_remote_copy(
            src_ref=part.at[l, :, cols(full, b)],
            dst_ref=full.at[l, pair, side, :, cols(full, b)],
            send_sem=seq_s.at[l, w, d], recv_sem=seq_r.at[l, w, d],
            device_id={"seq": lax.rem(i + 2 * d, n)}, device_id_type=MESH)

    def own_copy(l, w):
        part, full = weights[w]
        return pltpu.make_async_copy(
            part.at[l, :, cols(full, b)], full.at[l, pair, side, :, cols(full, b)], own_sem.at[l, w])

    def par_copy(l, w):
        part, full = weights[w]
        where = full.at[l, :, side, :, cols(full, b)]
        return pltpu.make_async_remote_copy(
            src_ref=where, dst_ref=where, send_sem=par_s.at[l, w], recv_sem=par_r.at[l, w],
            device_id={"seq": partner}, device_id_type=MESH)

    def bat_copy(l, w, m, o, parity):
        part, full = weights[w]
        quarter = b
        for bit in masks:
            if o & bit:
                quarter = flip(quarter, bit)
        which = lax.rem(side + parity, 2)
        where = full.at[l, :, which, :, cols(full, quarter)]
        return pltpu.make_async_remote_copy(
            src_ref=where, dst_ref=where,
            send_sem=bat_s.at[l, w, o + m, parity], recv_sem=bat_r.at[l, w, o + m, parity],
            device_id={"batch": flip(b, m)}, device_id_type=MESH)

    def act_copy(slot, c):
        source = (half, 0, half)[slot]
        hop = (2, 1, 1)[slot]
        return pltpu.make_async_remote_copy(
            src_ref=sig.at[pl.ds(source + c * chunk, chunk)],
            dst_ref=sbuf.at[pl.ds(slot * half + c * chunk, chunk)],
            send_sem=act_s.at[slot, c], recv_sem=act_r.at[slot, c],
            device_id={"seq": lax.rem(i + hop, n)}, device_id_type=MESH)

    def relay_copy(c):
        return pltpu.make_async_remote_copy(
            src_ref=sbuf.at[pl.ds(c * chunk, chunk)],
            dst_ref=sbuf.at[pl.ds(2 * half + c * chunk, chunk)],
            send_sem=act_s.at[2, c], recv_sem=act_r.at[2, c],
            device_id={"seq": partner}, device_id_type=MESH)

    relays = jnp.logical_and(side == 1, i >= 2)

    def relay(c):
        @pl.when(relays)
        def _():
            act_copy(0, c).wait_recv()
            relay_copy(c).start()

    def act_sends(slot):
        if slot == 2:
            return side == 0
        return i + (2, 1)[slot] < n

    def act_wait(slot, c):
        if slot == 0:
            pl.when(jnp.logical_and(side == 0, i >= 2))(act_copy(0, c).wait_recv)
        else:
            pl.when(i >= 1)(act_copy(slot, c).wait_recv)

    def seq_start(l):
        def go(d, _):
            for w in both:
                seq_copy(l, w, d).start()
            return 0
        lax.fori_loop(1, pairs, go, 0)

    def pair_start(l):
        def go(d, _):
            for w in both:
                seq_copy(l, w, d).wait_recv()
            return 0
        lax.fori_loop(1, pairs, go, 0)
        for w in both:
            own_copy(l, w).wait()
        for w in both:
            par_copy(l, w).start()
        for s in range(len(stages)):
            bat_start(l, s, 0, 0)

    stages = [(m, [o for o in range(nb) if all(o & x == 0 or x > m for x in masks)]) for m in masks]

    def bat_start(l, s, index, parity):
        m, held = stages[s]
        for w in both:
            bat_copy(l, w, m, held[index], parity).start()

    def bat_start_other(l):
        for w in both:
            par_copy(l, w).wait_recv()
        for s in range(len(stages)):
            bat_start(l, s, 0, 1)

    def bat_pass(l):
        for s, (m, held) in enumerate(stages):
            for index, o in enumerate(held):
                for parity in range(2):
                    for w in both:
                        bat_copy(l, w, m, o, parity).wait_recv()
                    for later in range(s + 1, len(stages)):
                        bat_start(l, later, stages[later][1].index(o + m), parity)

    for l in range(layers):
        for w in both:
            own_copy(l, w).start()
    if not gather_blend:
        blend = pltpu.make_async_copy(bw, bfull, own_sem.at[0, 1])
        blend.start()

    pl.semaphore_wait(barrier, n - 1 + len(masks))
    seq_start(0)
    for slot in (0, 2, 1):
        @pl.when(act_sends(slot))
        def _():
            for c in range(CHUNKS):
                act_copy(slot, c).start()

    @pl.when(i == 0)
    def _():
        sbuf[pl.ds(half, rows), :] = jnp.zeros((rows, channels), sbuf.dtype)

    @pl.when(i < 2)
    def _():
        sbuf[pl.ds(0, half), :] = jnp.zeros((half, channels), sbuf.dtype)

    seq_start(1)

    def layer(l, src, dst, shift, start, c):
        kernel_rows = kfull.at[l].reshape(n * kw.shape[1], kfull.shape[-1])
        blend_rows = bfull.at[l].reshape(channels, channels) if gather_blend else bfull.at[l]

        def step(t, _):
            for u in range(2):
                at = pl.multiple_of(start + c * chunk + (2 * t + u) * TILE, TILE)
                now = src[pl.ds(at + shift, TILE), :]
                late = src[pl.ds(at, TILE), :]
                pre = jnp.dot(late, kernel_rows[:channels, :], preferred_element_type=jnp.float32)
                pre += jnp.dot(now, kernel_rows[channels:, :], preferred_element_type=jnp.float32)
                gate = 0.5 * jnp.tanh(0.5 * pre[:, channels:]) + 0.5
                gated = (jnp.tanh(pre[:, :channels]) * gate).astype(jnp.bfloat16)
                mix = jnp.dot(gated, blend_rows[...], preferred_element_type=jnp.float32)
                dst[pl.ds(at, TILE), :] = (now.astype(jnp.float32) + mix).astype(jnp.bfloat16)
            return 0

        lax.fori_loop(0, chunk // (2 * TILE), step, 0)

    done = []

    def write(l, ref, start, c, place):
        copy = pltpu.make_async_copy(
            ref.at[pl.ds(start + c * chunk, chunk)], out.at[l, pl.ds(place * half + c * chunk, chunk)],
            out_sem.at[l, place, c])
        copy.start()
        done.append(copy)

    pair_start(0)
    relay(0)
    bat_start_other(0)
    bat_pass(0)
    load.wait()
    if not gather_blend:
        blend.wait()
    for c in range(CHUNKS):
        layer(0, sbuf, hbuf, half, 3 * half, c)
        write(0, hbuf, 3 * half, c, 1)
        if c == 0:
            for later in range(1, CHUNKS):
                relay(later)
            pair_start(1)
    bat_start_other(1)
    for c in range(CHUNKS):
        act_wait(2, c)
        layer(0, sbuf, hbuf, half, 2 * half, c)
        write(0, hbuf, 2 * half, c, 0)
    bat_pass(1)
    for c in range(CHUNKS):
        act_wait(1, c)
        layer(0, sbuf, hbuf, half, half, c)
        layer(1, hbuf, obuf, rows, half, c)
        write(1, obuf, half, c, 1)
    for c in range(CHUNKS):
        act_wait(0, c)
        layer(0, sbuf, hbuf, half, 0, c)
        layer(1, hbuf, obuf, rows, 0, c)
        write(1, obuf, 0, c, 0)

    def seq_sent(d, _):
        for l in range(layers):
            for w in both:
                seq_copy(l, w, d).wait_send()
        return 0

    lax.fori_loop(1, pairs, seq_sent, 0)
    for l in range(layers):
        for w in both:
            par_copy(l, w).wait_send()
        for m, held in stages:
            for o in held:
                for parity in range(2):
                    for w in both:
                        bat_copy(l, w, m, o, parity).wait_send()
    for slot in range(3):
        @pl.when(act_sends(slot))
        def _():
            for c in range(CHUNKS):
                act_copy(slot, c).wait_send()

    @pl.when(relays)
    def _():
        for c in range(CHUNKS):
            relay_copy(c).wait_send()
    for copy in done:
        copy.wait()


def per_device(n, nb, signal, kernel_weight_stack, blend_weight_stack):
    rows, channels = signal.shape
    layers, part_rows, width = kernel_weight_stack.shape
    gather_blend = blend_weight_stack.shape[1] % 16 == 0
    if not gather_blend:
        blend_weight_stack = lax.all_gather(blend_weight_stack, "seq", axis=1, tiled=True)
    blend_shape = (layers, channels, channels)
    if gather_blend:
        blend_shape = (layers, n // 2, 2, blend_weight_stack.shape[1], channels)
    half = rows // 2
    dma = pltpu.SemaphoreType.DMA
    any_space = pl.BlockSpec(memory_space=pl.ANY)
    return pl.pallas_call(
        functools.partial(kernel, n, nb, gather_blend),
        out_shape=jax.ShapeDtypeStruct((layers, rows, channels), signal.dtype),
        in_specs=[any_space] * 3,
        out_specs=any_space,
        scratch_shapes=[
            pltpu.VMEM((5 * half, channels), signal.dtype),
            pltpu.VMEM((4 * half, channels), signal.dtype),
            pltpu.VMEM((rows, channels), signal.dtype),
            pltpu.VMEM((layers, n // 2, 2, part_rows, width), signal.dtype),
            pltpu.VMEM(blend_shape, signal.dtype),
            dma((layers, 2, n // 2)), dma((layers, 2, n // 2)),
            dma((layers, 2)), dma((layers, 2)),
            dma((layers, 2, nb, 2)), dma((layers, 2, nb, 2)),
            dma((3, CHUNKS)), dma((3, CHUNKS)),
            dma((layers, 2)), dma, dma((layers, 2, CHUNKS)),
        ],
        compiler_params=pltpu.CompilerParams(
            collective_id=0, has_side_effects=True, vmem_limit_bytes=62 * 2**20),
        cost_estimate=pl.CostEstimate(
            flops=3 * 2 * rows * channels * (2 * width + channels),
            bytes_accessed=2 * rows * channels * 2 * 3, transcendentals=3 * rows * width),
    )(signal, kernel_weight_stack, blend_weight_stack)


def solution(mesh):
    return jax.shard_map(
        functools.partial(per_device, mesh.shape["seq"], mesh.shape["batch"]),
        mesh=mesh,
        in_specs=(P(("batch", "seq"), None), P(None, "seq", None), P(None, "seq", None)),
        out_specs=P(None, ("batch", "seq"), None),
        check_vma=False,
    )
```

time: 140 us -> 118 us (0.84)
  the two profiles are of different devices: /device:TPU:26 before, /device:TPU:9 now
where the time goes in v2:
time: 118 us
  Pallas kernels  113 us (96%)
  local copies, waits for them, and re-layouts  4.47 us (4%)
    pallas_call x1, Pallas kernels, per_device(): pl.pallas_call(functools.partial(kernel, n, nb, gather_blend), out_shape=...  113 us
    unnamed x1, local copies, waits for them, and re-layouts  4.47 us

profile of v2, /device:TPU:9, one launch (start us, length us, event | category | flops | bytes accessed | tf_op | source)
XLA Modules:
  0.0 117.7 jit_solution(10767913623551810503)
XLA Ops:
  0.0 113.2 %shard_map.37 = bf16[2,2048,512]{2,1,0:T(8,128)(2,1)} custom-call(bf16[2048,512]{1,0:T(8,128)(2,1)} %sig.1, bf16[2,128,1024]{2,1,0:T(8,128)(2,1)} %kw.1, bf16[2,64,512]{2,1,0:T(8,128)(2,1)} %bw.1), custom_call_target="tpu_custom_call" | custom-call | flops 16106127360 | bytes 12582912 | tf_op jit(solution)/shard_map/pallas_call | solution.py:288
  113.2 4.5 %copy.5 = bf16[2,2048,512]{2,1,0:T(8,128)(2,1)} copy(bf16[2,2048,512]{2,1,0:T(8,128)(2,1)} %shard_map.37) | data formatting | bytes 8388608

commit v3 on v2

--- a/solution.py
+++ b/solution.py
@@ -169,7 +169,9 @@
 
     pl.semaphore_wait(barrier, n - 1 + len(masks))
     seq_start(0)
-    for slot in (0, 2, 1):
+    seq_start(1)
+
+    def act_start(slot):
         @pl.when(act_sends(slot))
         def _():
             for c in range(CHUNKS):
@@ -182,8 +184,6 @@
     @pl.when(i < 2)
     def _():
         sbuf[pl.ds(0, half), :] = jnp.zeros((half, channels), sbuf.dtype)
-
-    seq_start(1)
 
     def layer(l, src, dst, shift, start, c):
         kernel_rows = kfull.at[l].reshape(n * kw.shape[1], kfull.shape[-1])
@@ -214,9 +214,12 @@
         done.append(copy)
 
     pair_start(0)
+    act_start(0)
+    bat_start_other(0)
+    act_start(2)
+    act_start(1)
+    bat_pass(0)
     relay(0)
-    bat_start_other(0)
-    bat_pass(0)
     load.wait()
     if not gather_blend:
         blend.wait()

time: 118 us -> 117 us (level)
  no operation moved by 1% of the time
where the time goes in v3:
time: 117 us
  Pallas kernels  113 us (97%)
  local copies, waits for them, and re-layouts  4.47 us (4%)
    pallas_call x1, Pallas kernels, per_device(): pl.pallas_call(functools.partial(kernel, n, nb, gather_blend), out_shape=...  113 us
    unnamed x1, local copies, waits for them, and re-layouts  4.47 us

profile of v3, /device:TPU:9, one launch (start us, length us, event | category | flops | bytes accessed | tf_op | source)
XLA Modules:
  0.0 117.1 jit_solution(10529849199931325498)
XLA Ops:
  0.0 112.6 %shard_map.37 = bf16[2,2048,512]{2,1,0:T(8,128)(2,1)} custom-call(bf16[2048,512]{1,0:T(8,128)(2,1)} %sig.1, bf16[2,128,1024]{2,1,0:T(8,128)(2,1)} %kw.1, bf16[2,64,512]{2,1,0:T(8,128)(2,1)} %bw.1), custom_call_target="tpu_custom_call" | custom-call | flops 16106127360 | bytes 12582912 | tf_op jit(solution)/shard_map/pallas_call | solution.py:291
  112.6 4.5 %copy.5 = bf16[2,2048,512]{2,1,0:T(8,128)(2,1)} copy(bf16[2,2048,512]{2,1,0:T(8,128)(2,1)} %shard_map.37) | data formatting | bytes 8388608
